TPU v7x, 32 devices: a whole 2x2x4 slice. The times are simulated.
32 devices in a mesh: batch: 2 (over x), seq: 16 (over z, y, core).
Axes of the slice: x: 2, y: 2, z: 4, core: 2. Of those that a mesh axis runs over, the one named last changes fastest.
Arguments:
- signal: bfloat16 [2, 262144, 384], P('batch', 'seq'), may hold values from -6 to 6
- conv_weight: float32 [4, 384], replicated, may hold values from -2.5 to 2.5
- first_factor: bfloat16 [512, 512, 512], P('seq'), may hold values from -0.25 to 0.25
- second_factor: bfloat16 [512, 512, 512], P('seq'), may hold values from -0.25 to 0.25
- grad_output: bfloat16 [2, 262144, 384], P('batch', 'seq'), may hold values from -3 to 3
Outputs:
- grad_signal: bfloat16 [2, 262144, 384], P('batch', 'seq')
- grad_first: bfloat16 [512, 512, 512], P('seq', 'batch')
- grad_second: bfloat16 [512, 512, 512], P('seq', 'batch')
All inputs are finite; a program needn't handle non-finite values.
Results may differ from a plain program's by a relative error of at most 0.0065.
Values may be sent and summed in bfloat16 or wider, within the bound.
No kernel may reach another device: no remote copies, remote signals or barrier semaphores. Data moves between devices by JAX's collectives and lax.ppermute only.
A program may use at most 320 MiB of HBM per device.

v0:
```python
import functools

import jax
import jax.numpy as jnp
from jax import lax
from jax.experimental import pallas as pl
from jax.experimental.pallas import tpu as pltpu
from jax.sharding import PartitionSpec as P

ROW_TILE = 16
VMEM = 60 * 2**20
WEIGHT = 1


def passed_along(value, axis, steps):
    count = lax.axis_size(axis)
    initial, last = (max(0, -steps), min(count, count - steps))
    return lax.ppermute(value, axis, [(source, source + steps) for source in range(initial, last)])


def cuts(total, sizes):
    if sum(sizes) != total:
        sizes = (total,)
    return [(sum(sizes[:n]), size) for n, size in enumerate(sizes)]


def per_step(blocks, start=0):
    return next(n for n in (4, 2, 1) if blocks % n == 0 and start % n == 0)


def split_product_kernel(factor_ref, rows_ref, *out_refs):
    devices = out_refs[0].shape[0]
    for n in range(factor_ref.shape[0]):
        product = lax.dot_general(
            factor_ref[n], rows_ref[n], (((0,), (0,)), ((), ())), preferred_element_type=jnp.float32
        ).astype(jnp.bfloat16)
        dealt = product.reshape(devices, product.shape[0] // devices, product.shape[1])
        start = 0
        for out_ref in out_refs:
            size = out_ref.shape[2]
            out_ref[:, n] = dealt[:, start : start + size]
            start += size


def split_product(factor, rows, devices, pieces):
    blocks, depth, width = factor.shape
    channels = rows.shape[2]
    if any(size % ROW_TILE for _, size in pieces):
        product = jnp.einsum("kmi,kmd->kid", factor, rows, preferred_element_type=jnp.float32)
        product = product.astype(jnp.bfloat16).reshape(blocks, devices, width // devices, channels)
        return [
            product[:, :, start : start + size].transpose(1, 0, 2, 3) for start, size in pieces
        ]
    step = per_step(blocks)
    return pl.pallas_call(
        split_product_kernel,
        grid=(blocks // step,),
        in_specs=[
            pl.BlockSpec((step, depth, width), lambda k: (k, 0, 0)),
            pl.BlockSpec((step, depth, channels), lambda k: (k, 0, 0)),
        ],
        out_specs=[
            pl.BlockSpec((devices, step, size, channels), lambda k: (0, k, 0, 0)) for _, size in pieces
        ],
        out_shape=[
            jax.ShapeDtypeStruct((devices, blocks, size, channels), jnp.bfloat16) for _, size in pieces
        ],
        compiler_params=pltpu.CompilerParams(vmem_limit_bytes=VMEM),
        cost_estimate=pl.CostEstimate(
            flops=2 * blocks * depth * width * channels,
            bytes_accessed=2 * blocks * (depth * width + depth * channels + width * channels),
            transcendentals=0,
        ),
    )(factor, rows)


def outer_kernel(half_ref, left_ref, right_ref, *refs):
    out_ref = refs[-1]
    channels = left_ref.shape[-1]
    for n in range(left_ref.shape[0]):
        right = right_ref[n] if len(right_ref.shape) == 3 else right_ref[:, n].reshape(-1, channels)
        product = lax.dot_general(
            left_ref[n], right, (((1,), (1,)), ((), ())), preferred_element_type=jnp.float32
        ).astype(jnp.bfloat16)
        if len(refs) > 1:
            total = product.astype(jnp.float32) + refs[0][n].astype(jnp.float32)
            product = total.astype(jnp.bfloat16)
        out_ref[n] = product


def outer(half, left, right, start, received=None, into=None, total=None):
    halves = lax.axis_size("batch")
    rows, channels = left.shape[1] // halves, left.shape[2]
    if right.ndim == 4 and right.shape[2] % ROW_TILE:
        right = right.transpose(1, 0, 2, 3).reshape(right.shape[1], -1, channels)
    if right.ndim == 4:
        devices, blocks, part, _ = right.shape
        cols = devices * part
        step = per_step(blocks, start)
        right_spec = pl.BlockSpec((devices, step, part, channels), lambda b, h: (0, b, 0, 0))
        left_at, right_at = start // step, 0
    else:
        blocks, cols = min(left.shape[0], right.shape[0]), right.shape[1]
        step = per_step(blocks, start)
        left_at = start // step if left.shape[0] > blocks else 0
        right_at = start // step if right.shape[0] > blocks else 0
        right_spec = pl.BlockSpec((step, cols, channels), lambda b, h: (b + right_at, 0, 0))
    in_specs = [pl.BlockSpec((step, rows, channels), lambda b, h: (b + left_at, h[0], 0)), right_spec]
    args, aliases, out_at, out_blocks = [half, left, right], {}, 0, blocks
    if received is not None:
        in_specs.append(pl.BlockSpec((step, rows, cols), lambda b, h: (b, 0, 0)))
        args.append(received)
        out_at, out_blocks = start // step, total
        if into is not None:
            in_specs.append(pl.BlockSpec(memory_space=pl.ANY))
            aliases = {len(args): 0}
            args.append(into)
    return pl.pallas_call(
        outer_kernel,
        grid_spec=pltpu.PrefetchScalarGridSpec(
            num_scalar_prefetch=1,
            grid=(blocks // step,),
            in_specs=in_specs,
            out_specs=pl.BlockSpec((step, rows, cols), lambda b, h: (b + out_at, 0, 0)),
        ),
        out_shape=jax.ShapeDtypeStruct((out_blocks, rows, cols), jnp.bfloat16),
        input_output_aliases=aliases,
        compiler_params=pltpu.CompilerParams(vmem_limit_bytes=VMEM),
        cost_estimate=pl.CostEstimate(
            flops=2 * blocks * rows * cols * channels,
            bytes_accessed=2 * blocks * (rows * cols + rows * channels + cols * channels),
            transcendentals=0,
        ),
    )(*args)


def back_kernel(factor_ref, rows_ref, slope_ref, out_ref):
    product = lax.dot_general(
        factor_ref[0], rows_ref[0], (((0,), (0,)), ((), ())), preferred_element_type=jnp.float32
    )
    out_ref[...] = (product * slope_ref[...]).astype(jnp.bfloat16)


def back(factor, rows, slope, start):
    blocks, depth, channels = rows.shape
    width = factor.shape[2]
    return pl.pallas_call(
        back_kernel,
        grid=(blocks,),
        in_specs=[
            pl.BlockSpec((1, depth, width), lambda b: (b + start, 0, 0)),
            pl.BlockSpec((1, depth, channels), lambda b: (b, 0, 0)),
            pl.BlockSpec((width, channels), lambda b: (b + start, 0)),
        ],
        out_specs=pl.BlockSpec((width, channels), lambda b: (b, 0)),
        out_shape=jax.ShapeDtypeStruct((blocks * width, channels), jnp.bfloat16),
        compiler_params=pltpu.CompilerParams(vmem_limit_bytes=VMEM),
        cost_estimate=pl.CostEstimate(
            flops=WEIGHT * 2 * blocks * depth * width * channels,
            bytes_accessed=WEIGHT * 2 * blocks * (depth * width + depth * channels + 3 * width * channels),
            transcendentals=0,
        ),
    )(factor, rows, slope)


def signal_kernel(cuts_, taps, *refs):
    pieces, firsts = refs[: len(cuts_)], refs[len(cuts_) : 2 * len(cuts_)]
    following_ref, weight_ref, out_ref = refs[2 * len(cuts_) :]
    block, last = pl.program_id(0), pl.num_programs(0) - 1

    def spread(rows, next_rows):
        rows = rows[...].astype(jnp.float32)
        extended = jnp.concatenate([rows, next_rows[...].astype(jnp.float32)], axis=0)
        total = weight_ref[0:1, :] * rows
        for r in range(1, taps):
            ahead = pltpu.roll(extended, extended.shape[0] - r, 0)[: rows.shape[0]]
            total += weight_ref[r : r + 1, :] * ahead
        out_ref[...] = total.astype(jnp.bfloat16)

    for n, (start, size) in enumerate(cuts_):
        end = start + size - 1

        @pl.when((block >= start) & (block < end))
        def _():
            spread(pieces[n], firsts[n])

        @pl.when(block == end)
        def _():
            spread(pieces[n], following_ref if n == len(cuts_) - 1 else firsts[n + 1])


def signal_back(grad_conv, following, conv_weight, cuts_, rows):
    channels = conv_weight.shape[1]
    blocks = sum(size for _, size in cuts_)
    following = jnp.pad(following, ((0, ROW_TILE - following.shape[0]), (0, 0)))
    step = rows // ROW_TILE

    def own(start, size):
        return lambda b: (jnp.clip(b - start, 0, size - 1), 0)

    def first_rows(start, size):
        return lambda b: (jnp.clip(b + 1 - start, 0, size - 1) * step, 0)

    return pl.pallas_call(
        functools.partial(signal_kernel, cuts_, conv_weight.shape[0]),
        grid=(blocks,),
        in_specs=[pl.BlockSpec((rows, channels), own(*cut)) for cut in cuts_]
        + [pl.BlockSpec((ROW_TILE, channels), first_rows(*cut)) for cut in cuts_]
        + [
            pl.BlockSpec((ROW_TILE, channels), lambda b: (0, 0)),
            pl.BlockSpec(conv_weight.shape, lambda b: (0, 0)),
        ],
        out_specs=pl.BlockSpec((rows, channels), lambda b: (b, 0)),
        out_shape=jax.ShapeDtypeStruct((blocks * rows, channels), jnp.bfloat16),
        compiler_params=pltpu.CompilerParams(vmem_limit_bytes=VMEM),
        cost_estimate=pl.CostEstimate(
            flops=WEIGHT * 8 * blocks * rows * channels,
            bytes_accessed=WEIGHT * 4 * blocks * rows * channels,
            transcendentals=0,
        ),
    )(*grad_conv, *grad_conv, following, conv_weight)


def body(signal, conv_weight, first_factor, second_factor, grad_output):
    _, tok_rows, channels = signal.shape
    blocks, block_order = first_factor.shape[0], first_factor.shape[1]
    col_blocks, block_count = second_factor.shape[0], second_factor.shape[1]
    tap_count = conv_weight.shape[0]
    devices = lax.axis_size("seq")
    mine = lax.axis_index("batch")[None]
    theirs = 1 - mine
    tail = tap_count - 1

    first_cuts = cuts(blocks, (16, 16))
    second_cuts = cuts(col_blocks, (14, 10, 8))

    tied = lax.optimization_barrier

    def swapped(part):
        return lax.ppermute(part, "batch", [(0, 1), (1, 0)])

    def exchanged(sent):
        return lax.all_to_all(sent, "seq", 0, 0, tiled=True)

    def ordered(rows, size):
        return rows.reshape(block_order, size, channels).transpose(1, 0, 2)

    previous = passed_along(signal[0, tok_rows - tail :, :], "seq", 1)
    upstream = grad_output.reshape(col_blocks, block_count, channels)
    outgoing = split_product(second_factor, upstream, devices, first_cuts)
    *outgoing, previous = tied((*outgoing, previous))

    arrived = exchanged(outgoing[0])
    padded_in = jnp.concatenate([previous, signal[0]], axis=0).astype(jnp.float32)
    conv_out = sum(
        conv_weight[r][None, :] * padded_in[tail - r : tail - r + tok_rows, :] for r in range(tap_count)
    )
    gate_val = jax.nn.sigmoid(conv_out)
    hidden = (conv_out * gate_val).astype(jnp.bfloat16).reshape(blocks, block_order, channels)
    slope = gate_val * (1.0 + conv_out * (1.0 - gate_val))
    mixed = jnp.einsum(
        "ikj,ijd->ikd", first_factor, hidden, preferred_element_type=jnp.float32
    ).astype(jnp.bfloat16)
    by_owner = mixed.reshape(blocks, devices, col_blocks, channels).transpose(1, 2, 0, 3)
    pieces = [by_owner[:, start : start + size] for start, size in second_cuts]
    arrived, hidden, slope, *rest = tied((arrived, hidden, slope, *pieces, *outgoing[1:]))
    pieces, rest = rest[: len(pieces)], rest[len(pieces) :]

    row_blocks, got_first, grad_conv = [], [], []
    for (start, size), sent in zip(first_cuts, rest):
        coming = exchanged(sent)
        rows, part = tied((ordered(arrived, size), outer(theirs, ordered(arrived, size), hidden, start)))
        got = swapped(part)
        back_rows = back(first_factor, rows, slope, start)
        row_blocks.append(rows)
        arrived, hidden, back_rows, got, *pieces = tied((coming, hidden, back_rows, got, *pieces))
        got_first.append(got)
        grad_conv.append(back_rows)

    columns = exchanged(pieces[0])
    start, size = first_cuts[-1]
    rows, part = tied((ordered(arrived, size), outer(theirs, ordered(arrived, size), hidden, start)))
    got = swapped(part)
    back_rows = back(first_factor, rows, slope, start)
    following = passed_along((grad_conv + [back_rows])[0][:tail, :], "seq", -1)
    columns, following, got, back_rows, *pieces = tied((columns, following, got, back_rows, *pieces[1:]))
    row_blocks.append(rows)
    got_first.append(got)
    grad_conv.append(back_rows)

    arrived_columns, got_second = [], []
    for step, (start, size) in enumerate(second_cuts):
        coming = exchanged(pieces[step]) if pieces[step:] else None
        part = outer(theirs, upstream, columns, start)
        arrived_columns.append(columns)
        if step == 0:
            following, part = tied((following, part))
            grad_signal = signal_back(grad_conv, following, conv_weight, first_cuts, block_order)
        got = swapped(part)
        if coming is not None:
            columns, grad_signal, got, *rest = tied((coming, grad_signal, got, *pieces[step + 1 :]))
            pieces[step + 1 :] = rest
        got_second.append(got)

    grad_first = grad_second = None
    for (start, _), rows, got in zip(first_cuts, row_blocks, got_first):
        grad_first = outer(mine, rows, hidden, start, got, grad_first, blocks)
    for (start, _), columns, got in zip(second_cuts, arrived_columns, got_second):
        grad_second = outer(mine, upstream, columns, start, got, grad_second, col_blocks)
    return (
        grad_signal[None],
        grad_first,
        grad_second,
    )


def solution(mesh):
    placed = (
        P("batch", "seq", None),
        P(),
        P("seq", None, None),
        P("seq", None, None),
        P("batch", "seq", None),
    )
    return jax.shard_map(
        body,
        mesh=mesh,
        in_specs=placed,
        out_specs=(P("batch", "seq", None), P("seq", "batch", None), P("seq", "batch", None)),
        check_vma=False,
    )
```

profile of v0, /device:TPU:0, one launch (start us, length us, event | category | flops | bytes accessed | tf_op | source)
XLA Modules:
  0.0 661.7 jit_solution(13279291725938110868)
XLA Ops:
  3.7 19.2 %shard_map.76 = (bf16[16,32,16,384]{3,2,1,0:T(8,128)(2,1)}, bf16[16,32,16,384]{3,2,1,0:T(8,128)(2,1)}) custom-call(bf16[32,512,512]{2,1,0:T(8,128)(2,1)} %factor_ref.3, bf16[32,512,384]{2,1,0:T(8,128)(2,1)} %bitcast.20), custom_call_target="tpu_custom_call" | custom-call | flops 6442450944 | bytes 41943040 | tf_op jit(solution)/shard_map/pallas_call | solution.py:55
  23.0 7.3 %all-to-all-start = ((bf16[16,32,16,384]{3,2,1,0:T(8,128)(2,1)}), bf16[16,32,16,384]{3,2,1,0:T(8,128)(2,1)}, u32[]{:S(2)}, u32[]{:S(2)}) async-start(bf16[16,32,16,384]{3,2,1,0:T(8,128)(2,1)} %get-tuple-element.43), calls=%async_computation | async-start | bytes 12582912 | tf_op jit(solution)/shard_map/all_to_all | solution.py:243
  30.3 14.2 %maximum_convert_fusion = f32[16387,384]{1,0:T(8,128)} fusion(bf16[16384,384]{1,0:T(8,128)(2,1)} %bitcast.41, bf16[3,384]{1,0:T(4,128)(2,1)S(1)} %collective-permute-done), kind=kLoop, calls=%fused_computation.10 | loop fusion | flops 25170432 | bytes 37755648 | tf_op jit(solution)/shard_map/convert_element_type | solution.py:254
  44.4 50.5 %add_multiply_fusion = (f32[16384,384]{1,0:T(8,128)}, f32[16384,384]{1,0:T(8,128)}) fusion(f32[16387,384]{1,0:T(8,128)} %maximum_convert_fusion, f32[384]{0:T(512)S(1)} %get-tuple-element.82, f32[384]{0:T(512)S(1)} %get-tuple-element.80, f32[384]{0:T(512)S(1)} %get-tuple-element.81, f32[384]{0:T(512)S(1)} %get-tuple-element.79), kind=kLoop, calls=%fused_computation.7 | loop fusion | flops 88080384 | bytes 151001088 | tf_op jit(solution)/shard_map/mul | solution.py:260
  94.9 15.5 %multiply_convert_fusion = bf16[16384,384]{1,0:T(8,128)(2,1)} fusion(f32[16384,384]{1,0:T(8,128)} %get-tuple-element.84), kind=kLoop, calls=%fused_computation.8 | loop fusion | flops 31457280 | bytes 37748736 | tf_op jit(solution)/shard_map/convert_element_type | solution.py:259
  110.4 17.8 %convert_bitcast_fusion = bf16[32,512,384]{1,2,0:T(8,128)(2,1)} fusion(bf16[32,512,384]{2,1,0:T(8,128)(2,1)} %bitcast.27, bf16[32,512,512]{2,1,0:T(8,128)(2,1)} %factor_ref.5), kind=kOutput, calls=%fused_computation.11 | convolution fusion | flops 6448742400 | bytes 41943040 | tf_op jit(solution)/shard_map/ikj,ijd->ikd/dot_general | solution.py:261
  128.2 16.8 %copy.12 = bf16[32,512,384]{2,0,1:T(8,128)(2,1)} copy(bf16[32,512,384]{1,2,0:T(8,128)(2,1)} %convert_bitcast_fusion) | data formatting | bytes 25165824 | tf_op jit(solution)/shard_map/convert_element_type | solution.py:263
  145.0 5.6 slice.56
  159.0 13.6 %all-to-all-start.1 = ((bf16[16,32,16,384]{3,2,1,0:T(8,128)(2,1)}), bf16[16,32,16,384]{3,2,1,0:T(8,128)(2,1)}, u32[]{:S(2)}, u32[]{:S(2)}) async-start(bf16[16,32,16,384]{3,2,1,0:T(8,128)(2,1)} %get-tuple-element.46), calls=%async_computation.1 | async-start | bytes 12582912 | tf_op jit(solution)/shard_map/all_to_all | solution.py:243
  172.6 7.0 %copy.13 = bf16[16,32,16,384]{3,1,0,2:T(8,128)(2,1)} copy(bf16[16,32,16,384]{3,2,1,0:T(8,128)(2,1)} %all-to-all-done) | data formatting | bytes 12582912 | tf_op jit(solution)/shard_map/optimization_barrier | solution.py:266
  179.6 7.4 %shard_map.77 = bf16[16,256,512]{2,1,0:T(8,128)(2,1)} custom-call(s32[1]{0:T(128)S(6)} %sub.7.half_ref, bf16[16,512,384]{2,1,0:T(8,128)(2,1)} %bitcast.32, bf16[32,512,384]{2,1,0:T(8,128)(2,1)} %bitcast.28), custom_call_target="tpu_custom_call" | custom-call | flops 1610612736 | bytes 13631488 | tf_op jit(solution)/shard_map/pallas_call | solution.py:118
  188.5 18.5 %shard_map.78.refs_0_.refs_2_ = bf16[8192,384]{1,0:T(8,128)(2,1)} custom-call(bf16[32,512,512]{2,1,0:T(8,128)(2,1)} %factor_ref.5, bf16[16,512,384]{2,1,0:T(8,128)(2,1)} %bitcast.33, f32[16384,384]{1,0:T(8,128)} %get-tuple-element.50.slope_ref), custom_call_target="tpu_custom_call" | custom-call | flops 3221225472 | bytes 33554432 | tf_op jit(solution)/shard_map/pallas_call | solution.py:147
  207.0 73.1 %collective-permute-done.1.refs_0_ = bf16[16,256,512]{2,1,0:T(8,128)(2,1)} collective-permute-done((bf16[16,256,512]{2,1,0:T(8,128)(2,1)}, bf16[16,256,512]{2,1,0:T(8,128)(2,1)}, u32[]{:S(2)}, u32[]{:S(2)}) %collective-permute-start.1) | collective-permute-done | bytes 4194336 | tf_op jit(solution)/shard_map/ppermute | solution.py:240
  280.1 6.6 %all-to-all-done.1 = bf16[16,32,16,384]{3,2,1,0:T(8,128)(2,1)} async-done(((bf16[16,32,16,384]{3,2,1,0:T(8,128)(2,1)}), bf16[16,32,16,384]{3,2,1,0:T(8,128)(2,1)}, u32[]{:S(2)}, u32[]{:S(2)}) %all-to-all-start.1) | async-done | bytes 6291488 | tf_op jit(solution)/shard_map/all_to_all | solution.py:243
  286.8 28.1 %all-to-all-start.2 = ((bf16[16,14,32,384]{3,2,1,0:T(8,128)(2,1)}), bf16[16,14,32,384]{3,2,1,0:T(8,128)(2,1)}, u32[]{:S(2)}, u32[]{:S(2)}) async-start(bf16[16,14,32,384]{3,2,1,0:T(8,128)(2,1)} %slice.56), calls=%async_computation.2 | async-start | bytes 11010048 | tf_op jit(solution)/shard_map/all_to_all | solution.py:243
  314.9 6.9 %copy.14 = bf16[16,32,16,384]{3,1,0,2:T(8,128)(2,1)} copy(bf16[16,32,16,384]{3,2,1,0:T(8,128)(2,1)} %all-to-all-done.1) | data formatting | bytes 12582912 | tf_op jit(solution)/shard_map/optimization_barrier | solution.py:276
  321.8 7.3 %shard_map.79 = bf16[16,256,512]{2,1,0:T(8,128)(2,1)} custom-call(s32[1]{0:T(128)S(6)} %sub.7.half_ref, bf16[16,512,384]{2,1,0:T(8,128)(2,1)} %bitcast.35, bf16[32,512,384]{2,1,0:T(8,128)(2,1)} %bitcast.29), custom_call_target="tpu_custom_call" | custom-call | flops 1610612736 | bytes 13631488 | tf_op jit(solution)/shard_map/pallas_call | solution.py:118
  332.6 18.5 %shard_map.80.refs_1_.refs_3_ = bf16[8192,384]{1,0:T(8,128)(2,1)} custom-call(bf16[32,512,512]{2,1,0:T(8,128)(2,1)} %factor_ref.5, bf16[16,512,384]{2,1,0:T(8,128)(2,1)} %bitcast.36, f32[16384,384]{1,0:T(8,128)} %get-tuple-element.50.slope_ref), custom_call_target="tpu_custom_call" | custom-call | flops 3221225472 | bytes 33554432 | tf_op jit(solution)/shard_map/pallas_call | solution.py:147
  351.0 71.2 %collective-permute-done.3.refs_0_ = bf16[16,256,512]{2,1,0:T(8,128)(2,1)} collective-permute-done((bf16[16,256,512]{2,1,0:T(8,128)(2,1)}, bf16[16,256,512]{2,1,0:T(8,128)(2,1)}, u32[]{:S(2)}, u32[]{:S(2)}) %collective-permute-start.3) | collective-permute-done | bytes 4194336 | tf_op jit(solution)/shard_map/ppermute | solution.py:240
  422.3 18.1 %all-to-all-start.3 = ((bf16[16,10,32,384]{3,2,1,0:T(8,128)(2,1)}), bf16[16,10,32,384]{3,2,1,0:T(8,128)(2,1)}, u32[]{:S(2)}, u32[]{:S(2)}) async-start(bf16[16,10,32,384]{3,2,1,0:T(8,128)(2,1)} %slice.57), calls=%async_computation.3 | async-start | bytes 7864320 | tf_op jit(solution)/shard_map/all_to_all | solution.py:243
  440.4 8.5 %shard_map.81 = bf16[14,256,512]{2,1,0:T(8,128)(2,1)} custom-call(s32[1]{0:T(128)S(6)} %sub.7.half_ref, bf16[32,512,384]{2,1,0:T(8,128)(2,1)} %bitcast.21, bf16[16,14,32,384]{3,2,1,0:T(8,128)(2,1)} %all-to-all-done.2.right_ref), custom_call_target="tpu_custom_call" | custom-call | flops 1409286144 | bytes 11927552 | tf_op jit(solution)/shard_map/pallas_call | solution.py:118
  451.0 26.4 %shard_map.82 = bf16[16384,384]{1,0:T(8,128)(2,1)} custom-call(bf16[8192,384]{1,0:T(8,128)(2,1)} %shard_map.78.refs_0_.refs_2_, bf16[8192,384]{1,0:T(8,128)(2,1)} %shard_map.80.refs_1_.refs_3_, bf16[8192,384]{1,0:T(8,128)(2,1)} %shard_map.78.refs_0_.refs_2_, bf16[8192,384]{1,0:T(8,128)(2,1)} %shard_map.80.refs_1_.refs_3_, bf16[16,384]{1,0:T(8,128)(2,1)} %pad.4.refs_4_, ...), custom_call_target="tpu_custom_call" | custom-call | flops 50331648 | bytes 25165824 | tf_op jit(solution)/shard_map/pallas_call | solution.py:204
  477.3 53.4 %collective-permute-done.4.refs_0_ = bf16[14,256,512]{2,1,0:T(8,128)(2,1)} collective-permute-done((bf16[14,256,512]{2,1,0:T(8,128)(2,1)}, bf16[14,256,512]{2,1,0:T(8,128)(2,1)}, u32[]{:S(2)}, u32[]{:S(2)}) %collective-permute-start.4) | collective-permute-done | bytes 3670048 | tf_op jit(solution)/shard_map/ppermute | solution.py:240
  530.8 5.8 all-to-all-start.4
  536.5 6.5 shard_map.83
  544.6 58.0 %collective-permute-done.5.refs_0_ = bf16[10,256,512]{2,1,0:T(8,128)(2,1)} collective-permute-done((bf16[10,256,512]{2,1,0:T(8,128)(2,1)}, bf16[10,256,512]{2,1,0:T(8,128)(2,1)}, u32[]{:S(2)}, u32[]{:S(2)}) %collective-permute-start.5) | collective-permute-done | bytes 2621472 | tf_op jit(solution)/shard_map/ppermute | solution.py:240
  609.9 8.2 %shard_map.84.refs_1_ = bf16[32,256,512]{2,1,0:T(8,128)(2,1)} custom-call(s32[1]{0:T(128)} %bitcast.10.half_ref, bf16[16,512,384]{2,1,0:T(8,128)(2,1)} %bitcast.34, bf16[32,512,384]{2,1,0:T(8,128)(2,1)} %bitcast.30, bf16[16,256,512]{2,1,0:T(8,128)(2,1)} %collective-permute-done.1.refs_0_), custom_call_target="tpu_custom_call" | custom-call | flops 1610612736 | bytes 13631488 | tf_op jit(solution)/shard_map/pallas_call | solution.py:118
  618.1 8.2 %shard_map.85 = bf16[32,256,512]{2,1,0:T(8,128)(2,1)} custom-call(s32[1]{0:T(128)} %bitcast.10.half_ref, bf16[16,512,384]{2,1,0:T(8,128)(2,1)} %bitcast.37, bf16[32,512,384]{2,1,0:T(8,128)(2,1)} %bitcast.31, bf16[16,256,512]{2,1,0:T(8,128)(2,1)} %collective-permute-done.3.refs_0_, ...), custom_call_target="tpu_custom_call", output_to_operand_aliasing={{}: (4, {})} | custom-call | flops 1610612736 | bytes 13631488 | tf_op jit(solution)/shard_map/pallas_call | solution.py:118
  626.3 9.5 %shard_map.87.refs_1_ = bf16[32,256,512]{2,1,0:T(8,128)(2,1)} custom-call(s32[1]{0:T(128)} %bitcast.10.half_ref, bf16[32,512,384]{2,1,0:T(8,128)(2,1)} %bitcast.24, bf16[16,14,32,384]{3,2,1,0:T(8,128)(2,1)} %all-to-all-done.2.right_ref, bf16[14,256,512]{2,1,0:T(8,128)(2,1)} %collective-permute-done.4.refs_0_), custom_call_target="tpu_custom_call" | custom-call | flops 1409286144 | bytes 11927552 | tf_op jit(solution)/shard_map/pallas_call | solution.py:118
  635.8 7.2 %shard_map.88.refs_1_ = bf16[32,256,512]{2,1,0:T(8,128)(2,1)} custom-call(s32[1]{0:T(128)} %bitcast.10.half_ref, bf16[32,512,384]{2,1,0:T(8,128)(2,1)} %bitcast.25, bf16[16,10,32,384]{3,2,1,0:T(8,128)(2,1)} %all-to-all-done.3.right_ref, bf16[10,256,512]{2,1,0:T(8,128)(2,1)} %collective-permute-done.5.refs_0_, ...), custom_call_target="tpu_custom_call", output_to_operand_aliasing={{}: (4, {})} | custom-call | flops 1006632960 | bytes 8519680 | tf_op jit(solution)/shard_map/pallas_call | solution.py:118
  643.0 12.7 %collective-permute-done.6.refs_0_ = bf16[8,256,512]{2,1,0:T(8,128)(2,1)S(1)} collective-permute-done((bf16[8,256,512]{2,1,0:T(8,128)(2,1)}, bf16[8,256,512]{2,1,0:T(8,128)(2,1)S(1)}, u32[]{:S(2)}, u32[]{:S(2)}) %collective-permute-start.6) | collective-permute-done | bytes 2097184 | tf_op jit(solution)/shard_map/ppermute | solution.py:240
  657.1 4.7 shard_map.89
  (26 shorter events, 28.7 us)
Async XLA Ops:
  0.6 22.3 %copy-start.2 = (f32[4,384]{1,0:T(4,128)S(1)}, f32[4,384]{1,0:T(4,128)}, u32[]{:S(2)}) copy-start(f32[4,384]{1,0:T(4,128)} %refs_5_.1) | copy-start | bytes 18436
  1.3 21.6 %collective-permute-start = (bf16[3,384]{1,0:T(4,128)(2,1)S(1)}, bf16[3,384]{1,0:T(4,128)(2,1)S(1)}, u32[]{:S(2)}, u32[]{:S(2)}) collective-permute-start(bf16[3,384]{1,0:T(4,128)(2,1)S(1)} %slice_bitcast_fusion), channel_id=1, source_target_pairs={{0,1},{1,2},{2,3},{3,4},{4,5},{5,6},{6,7},{7,8},{8,9},{9,10},{10,1... | collective-permute-start | bytes 6920 | tf_op jit(solution)/shard_map/ppermute | solution.py:18
  23.0 136.0 %all-to-all-start = ((bf16[16,32,16,384]{3,2,1,0:T(8,128)(2,1)}), bf16[16,32,16,384]{3,2,1,0:T(8,128)(2,1)}, u32[]{:S(2)}, u32[]{:S(2)}) async-start(bf16[16,32,16,384]{3,2,1,0:T(8,128)(2,1)} %get-tuple-element.43), calls=%async_computation | async-start | bytes 12582912 | tf_op jit(solution)/shard_map/all_to_all | solution.py:243
  159.0 127.8 %all-to-all-start.1 = ((bf16[16,32,16,384]{3,2,1,0:T(8,128)(2,1)}), bf16[16,32,16,384]{3,2,1,0:T(8,128)(2,1)}, u32[]{:S(2)}, u32[]{:S(2)}) async-start(bf16[16,32,16,384]{3,2,1,0:T(8,128)(2,1)} %get-tuple-element.46), calls=%async_computation.1 | async-start | bytes 12582912 | tf_op jit(solution)/shard_map/all_to_all | solution.py:243
  187.0 93.1 %collective-permute-start.1 = (bf16[16,256,512]{2,1,0:T(8,128)(2,1)}, bf16[16,256,512]{2,1,0:T(8,128)(2,1)}, u32[]{:S(2)}, u32[]{:S(2)}) collective-permute-start(bf16[16,256,512]{2,1,0:T(8,128)(2,1)} %shard_map.77), channel_id=1, source_target_pairs={{0,16},{16,0},{1,17},{17,1},{2,18},{18,2},{3,19},{19,3},{4,20},{20... | collective-permute-start | bytes 12582920 | tf_op jit(solution)/shard_map/ppermute | solution.py:240
  286.8 135.5 %all-to-all-start.2 = ((bf16[16,14,32,384]{3,2,1,0:T(8,128)(2,1)}), bf16[16,14,32,384]{3,2,1,0:T(8,128)(2,1)}, u32[]{:S(2)}, u32[]{:S(2)}) async-start(bf16[16,14,32,384]{3,2,1,0:T(8,128)(2,1)} %slice.56), calls=%async_computation.2 | async-start | bytes 11010048 | tf_op jit(solution)/shard_map/all_to_all | solution.py:243
  329.1 93.2 %collective-permute-start.3 = (bf16[16,256,512]{2,1,0:T(8,128)(2,1)}, bf16[16,256,512]{2,1,0:T(8,128)(2,1)}, u32[]{:S(2)}, u32[]{:S(2)}) collective-permute-start(bf16[16,256,512]{2,1,0:T(8,128)(2,1)} %shard_map.79), channel_id=1, source_target_pairs={{0,16},{16,0},{1,17},{17,1},{2,18},{18,2},{3,19},{19,3},{4,20},{20... | collective-permute-start | bytes 12582920 | tf_op jit(solution)/shard_map/ppermute | solution.py:240
  331.3 19.7 %collective-permute-start.2 = (bf16[3,384]{1,0:T(4,128)(2,1)S(1)}, bf16[3,384]{1,0:T(4,128)(2,1)S(1)}, u32[]{:S(2)}, u32[]{:S(2)}) collective-permute-start(bf16[3,384]{1,0:T(4,128)(2,1)S(1)} %slice.51), channel_id=1, source_target_pairs={{1,0},{2,1},{3,2},{4,3},{5,4},{6,5},{7,6},{8,7},{9,8},{10,9},{11,1... | collective-permute-start | bytes 6920 | tf_op jit(solution)/shard_map/ppermute | solution.py:18
  422.3 108.5 %all-to-all-start.3 = ((bf16[16,10,32,384]{3,2,1,0:T(8,128)(2,1)}), bf16[16,10,32,384]{3,2,1,0:T(8,128)(2,1)}, u32[]{:S(2)}, u32[]{:S(2)}) async-start(bf16[16,10,32,384]{3,2,1,0:T(8,128)(2,1)} %slice.57), calls=%async_computation.3 | async-start | bytes 7864320 | tf_op jit(solution)/shard_map/all_to_all | solution.py:243
  448.9 81.9 %collective-permute-start.4 = (bf16[14,256,512]{2,1,0:T(8,128)(2,1)}, bf16[14,256,512]{2,1,0:T(8,128)(2,1)}, u32[]{:S(2)}, u32[]{:S(2)}) collective-permute-start(bf16[14,256,512]{2,1,0:T(8,128)(2,1)} %shard_map.81), channel_id=1, source_target_pairs={{0,16},{16,0},{1,17},{17,1},{2,18},{18,2},{3,19},{19,3},{4,20},{20... | collective-permute-start | bytes 11010056 | tf_op jit(solution)/shard_map/ppermute | solution.py:240
  530.8 71.8 %all-to-all-start.4 = ((bf16[16,8,32,384]{3,2,1,0:T(8,128)(2,1)}), bf16[16,8,32,384]{3,2,1,0:T(8,128)(2,1)S(1)}, u32[]{:S(2)}, u32[]{:S(2)}) async-start(bf16[16,8,32,384]{3,2,1,0:T(8,128)(2,1)} %slice.58), calls=%async_computation.4 | async-start | bytes 6291456 | tf_op jit(solution)/shard_map/all_to_all | solution.py:243
  543.1 59.5 %collective-permute-start.5 = (bf16[10,256,512]{2,1,0:T(8,128)(2,1)}, bf16[10,256,512]{2,1,0:T(8,128)(2,1)}, u32[]{:S(2)}, u32[]{:S(2)}) collective-permute-start(bf16[10,256,512]{2,1,0:T(8,128)(2,1)} %shard_map.83), channel_id=1, source_target_pairs={{0,16},{16,0},{1,17},{17,1},{2,18},{18,2},{3,19},{19,3},{4,20},{20... | collective-permute-start | bytes 7864328 | tf_op jit(solution)/shard_map/ppermute | solution.py:240
  602.6 1.7 copy-start
  608.4 47.4 %collective-permute-start.6 = (bf16[8,256,512]{2,1,0:T(8,128)(2,1)}, bf16[8,256,512]{2,1,0:T(8,128)(2,1)S(1)}, u32[]{:S(2)}, u32[]{:S(2)}) collective-permute-start(bf16[8,256,512]{2,1,0:T(8,128)(2,1)} %shard_map.86), channel_id=1, source_target_pairs={{0,16},{16,0},{1,17},{17,1},{2,18},{18,2},{3,19},{19,3},{4,20},{20... | collective-permute-start | bytes 6291464 | tf_op jit(solution)/shard_map/ppermute | solution.py:240
  655.7 1.3 copy-start.1
where the time goes:
time: 668 us; the launch traced here: 662 us
  waiting for transfers between devices  275 us (41%)
  Pallas kernels  154 us (23%)
  starting transfers between devices  84 us (13%)
  other arithmetic  80.2 us (12%)
  local copies, waits for them, and re-layouts  49.7 us (7%)
  matrix products  17.8 us (3%)
    ppermute x5, waiting for transfers between devices, swapped(): return lax.ppermute(part, 'batch', [(0, 1), (1, 0)])  269 us
    all_to_all x5, starting transfers between devices, exchanged(): return lax.all_to_all(sent, 'seq', 0, 0, tiled=True)  72.9 us
    pallas_call x10, Pallas kernels, outer(): pl.pallas_call(outer_kernel, grid_spec=pltpu.PrefetchScalarGridSpec(num_s...  71.7 us
    mul x1, other arithmetic, body(): slope = gate_val * (1.0 + conv_out * (1.0 - gate_val))  50.5 us
    pallas_call x2, Pallas kernels, back(): pl.pallas_call(back_kernel, grid=(blocks,), in_specs=[pl.BlockSpec((1, de...  37 us
    pallas_call x1, Pallas kernels, signal_back(): pl.pallas_call(functools.partial(signal_kernel, cuts_, conv_weight.shape[...  26.4 us
    pallas_call x1, Pallas kernels, split_product(): pl.pallas_call(split_product_kernel, grid=(blocks // step,), in_specs=[pl...  19.2 us
    dot_general x1, matrix products, body(): jnp.einsum('ikj,ijd->ikd', first_factor, hidden, preferred_element_type=j...  17.8 us
  transfers between devices with their start and end apart: 12, of which 6 were waited for; matrix products, arithmetic and copies ran while one was open for 22% of the time, Pallas kernels for 22%

commit v1 on v0

v1 whole, which is shorter than its diff:
```python
import functools

import jax
import jax.numpy as jnp
from jax import lax
from jax.experimental import pallas as pl
from jax.experimental.pallas import tpu as pltpu
from jax.sharding import PartitionSpec as P

ROW_TILE = 16
VMEM = 64 * 2**20 - 2**18
WEIGHT = 1


def passed_along(value, axis, steps):
    count = lax.axis_size(axis)
    initial, last = (max(0, -steps), min(count, count - steps))
    return lax.ppermute(value, axis, [(source, source + steps) for source in range(initial, last)])


def cuts(total, sizes):
    if sum(sizes) != total:
        sizes = (total,)
    return [(sum(sizes[:n]), size) for n, size in enumerate(sizes)]


def per_step(blocks, start=0):
    return next(n for n in (4, 2, 1) if blocks % n == 0 and start % n == 0)


def split_product_kernel(factor_ref, rows_ref, out_ref):
    devices = out_ref.shape[0]
    for n in range(factor_ref.shape[0]):
        product = lax.dot_general(
            factor_ref[n], rows_ref[n], (((0,), (0,)), ((), ())), preferred_element_type=jnp.float32
        ).astype(jnp.bfloat16)
        out_ref[:, n] = product.reshape(devices, product.shape[0] // devices, product.shape[1])


def split_product(factor, rows, devices, start, size):
    _, depth, width = factor.shape
    channels = rows.shape[2]
    part = width // devices
    if part % ROW_TILE:
        product = jnp.einsum(
            "kmi,kmd->kid",
            factor[start : start + size],
            rows[start : start + size],
            preferred_element_type=jnp.float32,
        ).astype(jnp.bfloat16)
        return product.reshape(size, devices, part, channels).transpose(1, 0, 2, 3)
    step = per_step(size, start)
    at = start // step
    return pl.pallas_call(
        split_product_kernel,
        grid=(size // step,),
        in_specs=[
            pl.BlockSpec((step, depth, width), lambda k: (k + at, 0, 0)),
            pl.BlockSpec((step, depth, channels), lambda k: (k + at, 0, 0)),
        ],
        out_specs=pl.BlockSpec((devices, step, part, channels), lambda k: (0, k, 0, 0)),
        out_shape=jax.ShapeDtypeStruct((devices, size, part, channels), jnp.bfloat16),
        compiler_params=pltpu.CompilerParams(vmem_limit_bytes=VMEM),
        cost_estimate=pl.CostEstimate(
            flops=2 * size * depth * width * channels,
            bytes_accessed=2 * size * (depth * width + depth * channels + width * channels),
            transcendentals=0,
        ),
    )(factor, rows)


def outer_kernel(half_ref, left_ref, right_ref, *refs):
    out_ref = refs[-1]
    channels = left_ref.shape[-1]
    for n in range(left_ref.shape[0]):
        right = right_ref[n] if len(right_ref.shape) == 3 else right_ref[:, n].reshape(-1, channels)
        product = lax.dot_general(
            left_ref[n], right, (((1,), (1,)), ((), ())), preferred_element_type=jnp.float32
        ).astype(jnp.bfloat16)
        if len(refs) == 1:
            out_ref[n] = product
        else:
            total = product.astype(jnp.float32) + refs[0][n].astype(jnp.float32)
            _, groups, _, rows, cols = out_ref.shape
            out_ref[n, :, 0] = total.astype(jnp.bfloat16).reshape(groups, rows, cols)


def outer(half, left, right, left_start=0, right_start=0, size=None, target=None):
    halves = lax.axis_size("batch")
    rows, channels = left.shape[1] // halves, left.shape[2]
    if right.ndim == 4 and right.shape[2] % ROW_TILE:
        right = right.transpose(1, 0, 2, 3).reshape(right.shape[1], -1, channels)
    out_start = target[3] if target else 0
    step = next(n for n in (4, 2, 1) if not any(v % n for v in (size, left_start, right_start, out_start)))
    left_at, right_at, out_at = left_start // step, right_start // step, out_start // step
    if right.ndim == 4:
        devices, _, part, _ = right.shape
        cols = devices * part
        right_spec = pl.BlockSpec((devices, step, part, channels), lambda b, h: (0, b + right_at, 0, 0))
    else:
        cols = right.shape[1]
        right_spec = pl.BlockSpec((step, cols, channels), lambda b, h: (b + right_at, 0, 0))
    in_specs = [pl.BlockSpec((step, rows, channels), lambda b, h: (b + left_at, h[0], 0)), right_spec]
    args, aliases = [half, left, right], {}
    if target is None:
        shape, out_spec = (size, rows, cols), pl.BlockSpec((step, rows, cols), lambda b, h: (b, 0, 0))
    else:
        received, into, (blocks, groups, pieces), _, piece = target
        shape = (blocks, groups, pieces, rows // groups, cols)
        out_spec = pl.BlockSpec(
            (step, groups, 1, rows // groups, cols), lambda b, h: (b + out_at, 0, piece, 0, 0)
        )
        in_specs.append(pl.BlockSpec((step, rows, cols), lambda b, h: (b, 0, 0)))
        args.append(received)
        if into is not None:
            in_specs.append(pl.BlockSpec(memory_space=pl.ANY))
            aliases = {len(args): 0}
            args.append(into)
    return pl.pallas_call(
        outer_kernel,
        grid_spec=pltpu.PrefetchScalarGridSpec(
            num_scalar_prefetch=1, grid=(size // step,), in_specs=in_specs, out_specs=out_spec
        ),
        out_shape=jax.ShapeDtypeStruct(shape, jnp.bfloat16),
        input_output_aliases=aliases,
        compiler_params=pltpu.CompilerParams(vmem_limit_bytes=VMEM),
        cost_estimate=pl.CostEstimate(
            flops=2 * size * rows * cols * channels,
            bytes_accessed=2 * size * (rows * cols + rows * channels + cols * channels),
            transcendentals=0,
        ),
    )(*args)


def back_kernel(groups, factor_ref, slope_ref, *refs):
    *rows_refs, out_ref = refs
    blocks, depth, width = factor_ref.shape
    share = depth // groups // len(rows_refs)
    for n in range(blocks):
        factor = factor_ref[n].reshape(groups, len(rows_refs), share, width)
        total = sum(
            lax.dot_general(
                factor[:, piece].reshape(groups * share, width),
                rows_ref[n],
                (((0,), (0,)), ((), ())),
                preferred_element_type=jnp.float32,
            )
            for piece, rows_ref in enumerate(rows_refs)
        )
        at = pl.ds(n * width, width)
        out_ref[at] = (total * slope_ref[at]).astype(jnp.bfloat16)


def back(factor, pieces, slope, groups):
    blocks, depth, width = factor.shape
    channels = slope.shape[1]
    step = 2 if blocks % 2 == 0 else 1
    return pl.pallas_call(
        functools.partial(back_kernel, groups),
        grid=(blocks // step,),
        in_specs=[
            pl.BlockSpec((step, depth, width), lambda b: (b, 0, 0)),
            pl.BlockSpec((step * width, channels), lambda b: (b, 0)),
        ]
        + [pl.BlockSpec((step, *rows.shape[1:]), lambda b: (b, 0, 0)) for rows in pieces],
        out_specs=pl.BlockSpec((step * width, channels), lambda b: (b, 0)),
        out_shape=jax.ShapeDtypeStruct((blocks * width, channels), jnp.bfloat16),
        compiler_params=pltpu.CompilerParams(vmem_limit_bytes=VMEM),
        cost_estimate=pl.CostEstimate(
            flops=2 * blocks * depth * width * channels,
            bytes_accessed=2 * blocks * (depth * width + depth * channels + 3 * width * channels),
            transcendentals=0,
        ),
    )(factor, slope, *pieces)


def signal_kernel(cuts_, taps, *refs):
    pieces, firsts = refs[: len(cuts_)], refs[len(cuts_) : 2 * len(cuts_)]
    following_ref, weight_ref, out_ref = refs[2 * len(cuts_) :]
    block, last = pl.program_id(0), pl.num_programs(0) - 1

    def spread(rows, next_rows):
        rows = rows[...].astype(jnp.float32)
        extended = jnp.concatenate([rows, next_rows[...].astype(jnp.float32)], axis=0)
        total = weight_ref[0:1, :] * rows
        for r in range(1, taps):
            ahead = pltpu.roll(extended, extended.shape[0] - r, 0)[: rows.shape[0]]
            total += weight_ref[r : r + 1, :] * ahead
        out_ref[...] = total.astype(jnp.bfloat16)

    for n, (start, size) in enumerate(cuts_):
        end = start + size - 1

        @pl.when((block >= start) & (block < end))
        def _():
            spread(pieces[n], firsts[n])

        @pl.when(block == end)
        def _():
            spread(pieces[n], following_ref if n == len(cuts_) - 1 else firsts[n + 1])


def signal_back(grad_conv, following, conv_weight, cuts_, rows):
    channels = conv_weight.shape[1]
    blocks = sum(size for _, size in cuts_)
    following = jnp.pad(following, ((0, ROW_TILE - following.shape[0]), (0, 0)))
    step = rows // ROW_TILE

    def own(start, size):
        return lambda b: (jnp.clip(b - start, 0, size - 1), 0)

    def first_rows(start, size):
        return lambda b: (jnp.clip(b + 1 - start, 0, size - 1) * step, 0)

    return pl.pallas_call(
        functools.partial(signal_kernel, cuts_, conv_weight.shape[0]),
        grid=(blocks,),
        in_specs=[pl.BlockSpec((rows, channels), own(*cut)) for cut in cuts_]
        + [pl.BlockSpec((ROW_TILE, channels), first_rows(*cut)) for cut in cuts_]
        + [
            pl.BlockSpec((ROW_TILE, channels), lambda b: (0, 0)),
            pl.BlockSpec(conv_weight.shape, lambda b: (0, 0)),
        ],
        out_specs=pl.BlockSpec((rows, channels), lambda b: (b, 0)),
        out_shape=jax.ShapeDtypeStruct((blocks * rows, channels), jnp.bfloat16),
        compiler_params=pltpu.CompilerParams(vmem_limit_bytes=VMEM),
        cost_estimate=pl.CostEstimate(
            flops=WEIGHT * 8 * blocks * rows * channels,
            bytes_accessed=WEIGHT * 4 * blocks * rows * channels,
            transcendentals=0,
        ),
    )(*grad_conv, *grad_conv, following, conv_weight)


def body(signal, conv_weight, first_factor, second_factor, grad_output):
    _, tok_rows, channels = signal.shape
    blocks, block_order = first_factor.shape[0], first_factor.shape[1]
    col_blocks, block_count = second_factor.shape[0], second_factor.shape[1]
    tap_count = conv_weight.shape[0]
    devices = lax.axis_size("seq")
    mine = lax.axis_index("batch")[None]
    theirs = 1 - mine
    tail = tap_count - 1

    first_cuts = cuts(col_blocks, (16, 16))
    second_cuts = cuts(col_blocks, (13, 9, 6, 4))
    tied = lax.optimization_barrier

    def swapped(part):
        return lax.ppermute(part, "batch", [(0, 1), (1, 0)])

    def exchanged(sent):
        return lax.all_to_all(sent, "seq", 0, 0, tiled=True)

    def ordered(rows):
        return rows.reshape(-1, blocks, channels).transpose(1, 0, 2)

    previous = passed_along(signal[0, tok_rows - tail :, :], "seq", 1)
    upstream = grad_output.reshape(col_blocks, block_count, channels)
    sent = split_product(second_factor, upstream, devices, *first_cuts[0])
    sent, previous = tied((sent, previous))

    arrived = exchanged(sent)
    padded_in = jnp.concatenate([previous, signal[0]], axis=0).astype(jnp.float32)
    conv_out = sum(
        conv_weight[r][None, :] * padded_in[tail - r : tail - r + tok_rows, :] for r in range(tap_count)
    )
    later, conv_out = tied((upstream, conv_out))
    rest = [split_product(second_factor, later, devices, *cut) for cut in first_cuts[1:]]
    gate_val = jax.nn.sigmoid(conv_out)
    hidden = (conv_out * gate_val).astype(jnp.bfloat16).reshape(blocks, block_order, channels)
    slope = gate_val * (1.0 + conv_out * (1.0 - gate_val))
    mixed = jnp.einsum(
        "ikj,ijd->ikd", first_factor, hidden, preferred_element_type=jnp.float32
    ).astype(jnp.bfloat16)
    by_owner = mixed.reshape(blocks, devices, col_blocks, channels).transpose(1, 2, 0, 3)
    pieces = [by_owner[:, start : start + size] for start, size in second_cuts]
    arrived, hidden, slope, *rest = tied((arrived, hidden, slope, *pieces, *rest))
    pieces, rest = rest[: len(pieces)], rest[len(pieces) :]

    shape_first = (blocks, devices // lax.axis_size("batch"), len(first_cuts))
    row_pieces, got_first, grad_first = [], [], None
    for sent in rest:
        coming = exchanged(sent)
        rows = ordered(arrived)
        got = swapped(outer(theirs, rows, hidden, size=blocks))
        arrived, rows, got, hidden, *pieces = tied((coming, rows, got, hidden, *pieces))
        row_pieces.append(rows)
        got_first.append(got)

    columns = exchanged(pieces[0])
    rows = ordered(arrived)
    rows, part = tied((rows, outer(theirs, rows, hidden, size=blocks)))
    got = swapped(part)
    row_pieces.append(rows)
    grad_conv = back(first_factor, row_pieces, slope, devices)
    following = passed_along(grad_conv[:tail, :], "seq", -1)
    for piece, earlier in enumerate(got_first):
        grad_first = outer(
            mine, row_pieces[piece], hidden, size=blocks, target=(earlier, grad_first, shape_first, 0, piece)
        )
    state = (columns, following, got, grad_conv, *pieces[1:])
    if got_first:
        state += (grad_first,)
    state = tied(state)
    columns, following, got, grad_conv, *pieces = state[: 4 + len(pieces) - 1]
    if got_first:
        grad_first = state[-1]

    shape_second = (col_blocks, 1, 1)
    grad_second = grad_signal = None
    held = []
    last_first = (got, grad_first, shape_first, 0, len(first_cuts) - 1)
    summing = []

    def own_half(start, at, size, columns, got):
        return lambda into: outer(
            mine, upstream, columns, start, at, size, target=(got, into, shape_second, start, 0)
        )

    for step, (start, size) in enumerate(second_cuts):
        coming = exchanged(pieces[step]) if pieces[step:] else None
        back_size = 1 if coming is not None else 0
        early = size - back_size
        part = outer(theirs, upstream, columns, start, 0, early)
        late_part = outer(theirs, upstream, columns, start + early, early, back_size) if back_size else None
        got_late = [(s0, a0, n0, c0, swapped(p0)) for s0, a0, n0, c0, p0 in held]
        if got_late:
            part, sent_late = tied((part, got_late[0][4]))
            got_late = [(*got_late[0][:4], sent_late)]
        got = swapped(part)
        if step == 0:
            grad_first = outer(mine, row_pieces[-1], hidden, size=blocks, target=last_first)
            grad_signal = signal_back([grad_conv], following, conv_weight, [(0, blocks)], block_order)
        if coming is not None:
            for add in summing:
                grad_second = add(grad_second)
            summing = []
        if coming is not None:
            state = [coming, got, late_part, grad_signal, grad_first, *pieces[step + 1 :]]
            state += [entry[4] for entry in got_late]
            if grad_second is not None:
                state.append(grad_second)
            state = list(tied(tuple(state)))
            if grad_second is not None:
                grad_second = state.pop()
            got_late = [(*entry[:4], state.pop()) for entry in got_late[::-1]]
            following_columns, got, late_part, grad_signal, grad_first, *rest = state
            pieces[step + 1 :] = rest
            held = [(start + early, early, back_size, columns, late_part)]
        summing += [own_half(*entry) for entry in got_late] + [own_half(start, 0, early, columns, got)]
        if coming is not None:
            columns = following_columns
    for add in summing:
        grad_second = add(grad_second)
    grad_first = grad_first.reshape(blocks, -1, block_order)
    grad_second = grad_second.reshape(col_blocks, -1, block_count)
    return (
        grad_signal[None],
        grad_first,
        grad_second,
    )


def solution(mesh):
    placed = (
        P("batch", "seq", None),
        P(),
        P("seq", None, None),
        P("seq", None, None),
        P("batch", "seq", None),
    )
    return jax.shard_map(
        body,
        mesh=mesh,
        in_specs=placed,
        out_specs=(P("batch", "seq", None), P("seq", "batch", None), P("seq", "batch", None)),
        check_vma=False,
    )
```

time: 668 us -> 650 us (0.973)
  waiting for transfers between devices: 275 us -> 245 us
  Pallas kernels: 154 us -> 181 us
  starting transfers between devices: 84 us -> 73.4 us
    add x0 -> x1, other arithmetic: none -> 41.8 us  [body(): sum((conv_weight[r][None, :] * padded_in[tail - r:tail - r + tok_rows, :]...]
    pallas_call x10 -> x18, Pallas kernels: 71.7 us -> 106 us  [outer(): pl.pallas_call(outer_kernel, grid_spec=pltpu.PrefetchScalarGridSpec(num_s...]
    mul x1, other arithmetic: 50.5 us -> 23.5 us  [body(): slope = gate_val * (1.0 + conv_out * (1.0 - gate_val))]
    ppermute x5 -> x9, waiting for transfers between devices: 269 us -> 243 us  [swapped(): return lax.ppermute(part, 'batch', [(0, 1), (1, 0)])]
    convert_element_type x1 -> x0, other arithmetic: 15.5 us -> none  [body(): (conv_out * gate_val).astype(jnp.bfloat16)]
    all_to_all x5 -> x6, starting transfers between devices: 72.9 us -> 59.1 us  [exchanged(): return lax.all_to_all(sent, 'seq', 0, 0, tiled=True)]
    pallas_call x3, Pallas kernels: 56.2 us -> 48.4 us  [the longest x1 27.9 us: back(): pl.pallas_call(functools.partial(back_kernel, groups), grid=(blocks // st...]
    slice x3 -> x4, local copies, waits for them, and re-layouts: 14 us -> 15.8 us  [body(): pieces = [by_owner[:, start:start + size] for start, size in second_cuts]]
  transfers between devices with their start and end apart: 12 -> 17, of which waited for: 6 -> 9; matrix products, arithmetic and copies ran while one was open for 22% -> 23% of each run, Pallas kernels for 22% -> 27%
where the time goes in v1:
time: 650 us; the launch traced here: 647 us
  waiting for transfers between devices  245 us (38%)
  Pallas kernels  181 us (28%)
  other arithmetic  79.5 us (12%)
  starting transfers between devices  73.4 us (11%)
  local copies, waits for them, and re-layouts  50 us (8%)
  matrix products  17.8 us (3%)
    ppermute x9, waiting for transfers between devices, swapped(): return lax.ppermute(part, 'batch', [(0, 1), (1, 0)])  243 us
    pallas_call x18, Pallas kernels, outer(): pl.pallas_call(outer_kernel, grid_spec=pltpu.PrefetchScalarGridSpec(num_s...  106 us
    all_to_all x6, starting transfers between devices, exchanged(): return lax.all_to_all(sent, 'seq', 0, 0, tiled=True)  59.1 us
    add x1, other arithmetic, body(): sum((conv_weight[r][None, :] * padded_in[tail - r:tail - r + tok_rows, :]...  41.8 us
    pallas_call x1, Pallas kernels, back(): pl.pallas_call(functools.partial(back_kernel, groups), grid=(blocks // st...  27.9 us
    pallas_call x1, Pallas kernels, signal_back(): pl.pallas_call(functools.partial(signal_kernel, cuts_, conv_weight.shape[...  26.2 us
    mul x1, other arithmetic, body(): slope = gate_val * (1.0 + conv_out * (1.0 - gate_val))  23.5 us
    pallas_call x2, Pallas kernels, split_product(): pl.pallas_call(split_product_kernel, grid=(size // step,), in_specs=[pl.B...  20.5 us
  transfers between devices with their start and end apart: 17, of which 9 were waited for; matrix products, arithmetic and copies ran while one was open for 23% of the time, Pallas kernels for 27%

profile of v1, /device:TPU:0, one launch (start us, length us, event | category | flops | bytes accessed | tf_op | source)
XLA Modules:
  0.0 647.0 jit_solution(9685511916247732645)
XLA Ops:
  3.7 10.3 %shard_map.76 = bf16[16,16,32,384]{3,2,1,0:T(8,128)(2,1)} custom-call(bf16[32,512,512]{2,1,0:T(8,128)(2,1)} %factor_ref.4, bf16[32,512,384]{2,1,0:T(8,128)(2,1)} %bitcast.22), custom_call_target="tpu_custom_call" | custom-call | flops 3221225472 | bytes 20971520 | tf_op jit(solution)/shard_map/pallas_call | solution.py:54
  14.0 7.3 %all-to-all-start = ((bf16[16,16,32,384]{3,2,1,0:T(8,128)(2,1)}), bf16[16,16,32,384]{3,2,1,0:T(8,128)(2,1)}, u32[]{:S(2)}, u32[]{:S(2)}) async-start(bf16[16,16,32,384]{3,2,1,0:T(8,128)(2,1)} %shard_map.76), calls=%async_computation | async-start | bytes 12582912 | tf_op jit(solution)/shard_map/all_to_all | solution.py:253
  21.3 14.2 %maximum_convert_fusion = f32[16387,384]{1,0:T(8,128)} fusion(bf16[16384,384]{1,0:T(8,128)(2,1)} %bitcast.55, bf16[3,384]{1,0:T(4,128)(2,1)S(1)} %collective-permute-done), kind=kLoop, calls=%fused_computation.10 | loop fusion | flops 25170432 | bytes 37755648 | tf_op jit(solution)/shard_map/convert_element_type | solution.py:264
  35.5 41.8 %fusion = f32[16384,384]{1,0:T(8,128)} fusion(f32[16387,384]{1,0:T(8,128)} %maximum_convert_fusion, f32[384]{0:T(512)S(1)} %get-tuple-element.122, f32[384]{0:T(512)S(1)} %get-tuple-element.120, f32[384]{0:T(512)S(1)} %get-tuple-element.121, f32[384]{0:T(512)S(1)} %get-tuple-element.119), kind=kLoop, calls=%fused_computation.1 | loop fusion | flops 44040192 | bytes 125835264 | tf_op jit(solution)/shard_map/add | solution.py:265
  77.3 23.5 %add_multiply_fusion = (f32[16384,384]{1,0:T(8,128)}, bf16[16384,384]{1,0:T(8,128)(2,1)}) fusion(f32[16384,384]{1,0:T(8,128)} %fusion), kind=kLoop, calls=%fused_computation.7 | loop fusion | flops 56623104 | bytes 62914560 | tf_op jit(solution)/shard_map/mul | solution.py:272
  100.8 17.8 %convert_bitcast_fusion = bf16[32,512,384]{1,2,0:T(8,128)(2,1)} fusion(bf16[32,512,384]{2,1,0:T(8,128)(2,1)} %bitcast.38, bf16[32,512,512]{2,1,0:T(8,128)(2,1)} %factor_ref.5), kind=kOutput, calls=%fused_computation.11 | convolution fusion | flops 6448742400 | bytes 41943040 | tf_op jit(solution)/shard_map/ikj,ijd->ikd/dot_general | solution.py:273
  118.5 16.8 %copy.16 = bf16[32,512,384]{2,0,1:T(8,128)(2,1)} copy(bf16[32,512,384]{1,2,0:T(8,128)(2,1)} %convert_bitcast_fusion) | data formatting | bytes 25165824 | tf_op jit(solution)/shard_map/convert_element_type | solution.py:275
  151.1 10.3 %shard_map.77 = bf16[16,16,32,384]{3,2,1,0:T(8,128)(2,1)} custom-call(bf16[32,512,512]{2,1,0:T(8,128)(2,1)} %factor_ref.4, bf16[32,512,384]{2,1,0:T(8,128)(2,1)} %bitcast.23), custom_call_target="tpu_custom_call" | custom-call | flops 3221225472 | bytes 20971520 | tf_op jit(solution)/shard_map/pallas_call | solution.py:54
  161.3 6.0 all-to-all-start.1
  167.4 7.8 %copy.17 = bf16[16,16,32,384]{3,1,0,2:T(8,128)(2,1)} copy(bf16[16,16,32,384]{3,2,1,0:T(8,128)(2,1)} %all-to-all-done) | data formatting | bytes 12582912 | tf_op jit(solution)/shard_map/optimization_barrier | solution.py:278
  175.2 11.3 %shard_map.78 = bf16[32,128,512]{2,1,0:T(8,128)(2,1)} custom-call(s32[1]{0:T(128)S(6)} %sub.7.half_ref, bf16[32,256,384]{2,1,0:T(8,128)(2,1)} %bitcast.44, bf16[32,512,384]{2,1,0:T(8,128)(2,1)} %bitcast.39), custom_call_target="tpu_custom_call" | custom-call | flops 1610612736 | bytes 19922944 | tf_op jit(solution)/shard_map/pallas_call | solution.py:119
  188.0 91.6 %collective-permute-done.1.refs_0_ = bf16[32,128,512]{2,1,0:T(8,128)(2,1)} collective-permute-done((bf16[32,128,512]{2,1,0:T(8,128)(2,1)}, bf16[32,128,512]{2,1,0:T(8,128)(2,1)}, u32[]{:S(2)}, u32[]{:S(2)}) %collective-permute-start.1) | collective-permute-done | bytes 4194336 | tf_op jit(solution)/shard_map/ppermute | solution.py:250
  281.6 28.1 %all-to-all-start.2 = ((bf16[16,13,32,384]{3,2,1,0:T(8,128)(2,1)}), bf16[16,13,32,384]{3,2,1,0:T(8,128)(2,1)}, u32[]{:S(2)}, u32[]{:S(2)}) async-start(bf16[16,13,32,384]{3,2,1,0:T(8,128)(2,1)} %slice.60), calls=%async_computation.2 | async-start | bytes 10223616 | tf_op jit(solution)/shard_map/all_to_all | solution.py:253
  309.7 7.7 %copy.18 = bf16[16,16,32,384]{3,1,0,2:T(8,128)(2,1)} copy(bf16[16,16,32,384]{3,2,1,0:T(8,128)(2,1)} %all-to-all-done.1) | data formatting | bytes 12582912 | tf_op jit(solution)/shard_map/optimization_barrier | solution.py:287
  317.4 11.3 %shard_map.79 = bf16[32,128,512]{2,1,0:T(8,128)(2,1)} custom-call(s32[1]{0:T(128)S(6)} %sub.7.half_ref, bf16[32,256,384]{2,1,0:T(8,128)(2,1)} %bitcast.47, bf16[32,512,384]{2,1,0:T(8,128)(2,1)} %bitcast.40), custom_call_target="tpu_custom_call" | custom-call | flops 1610612736 | bytes 19922944 | tf_op jit(solution)/shard_map/pallas_call | solution.py:119
  330.2 27.9 %shard_map.80.refs_0_.refs_1_ = bf16[16384,384]{1,0:T(8,128)(2,1)} custom-call(bf16[32,512,512]{2,1,0:T(8,128)(2,1)} %factor_ref.5, f32[16384,384]{1,0:T(8,128)} %get-tuple-element.73.slope_ref, bf16[32,256,384]{2,1,0:T(8,128)(2,1)} %bitcast.45, bf16[32,256,384]{2,1,0:T(8,128)(2,1)} %bitcast.48), custom_call_target="tpu_custom_call" | custom-call | flops 6442450944 | bytes 67108864 | tf_op jit(solution)/shard_map/pallas_call | solution.py:158
  360.0 12.0 %shard_map.81.refs_1_ = bf16[32,8,2,16,512]{4,3,2,1,0:T(8,128)(2,1)} custom-call(s32[1]{0:T(128)} %bitcast.10.half_ref, bf16[32,256,384]{2,1,0:T(8,128)(2,1)} %bitcast.46, bf16[32,512,384]{2,1,0:T(8,128)(2,1)} %bitcast.41, bf16[32,128,512]{2,1,0:T(8,128)(2,1)} %collective-permute-done.1.refs_0_), custom_call_target="tpu_custom_call" | custom-call | flops 1610612736 | bytes 19922944 | tf_op jit(solution)/shard_map/pallas_call | solution.py:119
  372.0 49.8 %collective-permute-done.3.refs_0_ = bf16[32,128,512]{2,1,0:T(8,128)(2,1)} collective-permute-done((bf16[32,128,512]{2,1,0:T(8,128)(2,1)}, bf16[32,128,512]{2,1,0:T(8,128)(2,1)}, u32[]{:S(2)}, u32[]{:S(2)}) %collective-permute-start.3) | collective-permute-done | bytes 4194336 | tf_op jit(solution)/shard_map/ppermute | solution.py:250
  421.8 5.8 all-to-all-start.3
  427.6 6.6 %shard_map.82 = bf16[12,256,512]{2,1,0:T(8,128)(2,1)} custom-call(s32[1]{0:T(128)S(6)} %sub.7.half_ref, bf16[32,512,384]{2,1,0:T(8,128)(2,1)} %bitcast.24, bf16[16,13,32,384]{3,2,1,0:T(8,128)(2,1)} %all-to-all-done.2.right_ref), custom_call_target="tpu_custom_call" | custom-call | flops 1207959552 | bytes 10223616 | tf_op jit(solution)/shard_map/pallas_call | solution.py:119
  436.3 26.2 %shard_map.84 = bf16[16384,384]{1,0:T(8,128)(2,1)} custom-call(bf16[16384,384]{1,0:T(8,128)(2,1)} %shard_map.80.refs_0_.refs_1_, bf16[16384,384]{1,0:T(8,128)(2,1)} %shard_map.80.refs_0_.refs_1_, bf16[16,384]{1,0:T(8,128)(2,1)} %pad.4.refs_2_, f32[4,384]{1,0:T(4,128)} %refs_3_.1), custom_call_target="tpu_custom_call" | custom-call | flops 50331648 | bytes 25165824 | tf_op jit(solution)/shard_map/pallas_call | solution.py:215
  464.6 12.0 %shard_map.85 = bf16[32,8,2,16,512]{4,3,2,1,0:T(8,128)(2,1)} custom-call(s32[1]{0:T(128)} %bitcast.10.half_ref, bf16[32,256,384]{2,1,0:T(8,128)(2,1)} %bitcast.49, bf16[32,512,384]{2,1,0:T(8,128)(2,1)} %bitcast.42, bf16[32,128,512]{2,1,0:T(8,128)(2,1)} %collective-permute-done.3.refs_0_, ...), custom_call_target="tpu_custom_call", output_to_operand_aliasing={{}: (4, {})} | custom-call | flops 1610612736 | bytes 19922944 | tf_op jit(solution)/shard_map/pallas_call | solution.py:119
  476.6 28.3 %collective-permute-done.4.refs_0_ = bf16[12,256,512]{2,1,0:T(8,128)(2,1)} collective-permute-done((bf16[12,256,512]{2,1,0:T(8,128)(2,1)}, bf16[12,256,512]{2,1,0:T(8,128)(2,1)}, u32[]{:S(2)}, u32[]{:S(2)}) %collective-permute-start.4) | collective-permute-done | bytes 3145760 | tf_op jit(solution)/shard_map/ppermute | solution.py:250
  504.9 6.1 all-to-all-start.4
  512.5 7.4 %shard_map.86 = bf16[8,256,512]{2,1,0:T(8,128)(2,1)} custom-call(s32[1]{0:T(128)S(6)} %sub.7.half_ref, bf16[32,512,384]{2,1,0:T(8,128)(2,1)} %bitcast.26, bf16[16,9,32,384]{3,2,1,0:T(8,128)(2,1)} %all-to-all-done.3.right_ref), custom_call_target="tpu_custom_call" | custom-call | flops 805306368 | bytes 6815744 | tf_op jit(solution)/shard_map/pallas_call | solution.py:119
  523.5 7.2 %shard_map.88.refs_1_ = bf16[32,1,1,256,512]{4,3,2,1,0:T(8,128)(2,1)} custom-call(s32[1]{0:T(128)} %bitcast.10.half_ref, bf16[32,512,384]{2,1,0:T(8,128)(2,1)} %bitcast.28, bf16[16,13,32,384]{3,2,1,0:T(8,128)(2,1)} %all-to-all-done.2.right_ref, bf16[12,256,512]{2,1,0:T(8,128)(2,1)} %collective-permute-done.4.refs_0_), custom_call_target="tpu_custom_call" | custom-call | flops 1207959552 | bytes 10223616 | tf_op jit(solution)/shard_map/pallas_call | solution.py:119
  530.7 37.1 %collective-permute-done.6.refs_0_ = bf16[8,256,512]{2,1,0:T(8,128)(2,1)} collective-permute-done((bf16[8,256,512]{2,1,0:T(8,128)(2,1)}, bf16[8,256,512]{2,1,0:T(8,128)(2,1)}, u32[]{:S(2)}, u32[]{:S(2)}) %collective-permute-start.6) | collective-permute-done | bytes 2097184 | tf_op jit(solution)/shard_map/ppermute | solution.py:250
  567.8 5.8 all-to-all-start.5
  587.6 7.7 %shard_map.92.refs_1_ = bf16[32,1,1,256,512]{4,3,2,1,0:T(8,128)(2,1)} custom-call(s32[1]{0:T(128)} %bitcast.10.half_ref, bf16[32,512,384]{2,1,0:T(8,128)(2,1)} %bitcast.32, bf16[16,9,32,384]{3,2,1,0:T(8,128)(2,1)} %all-to-all-done.3.right_ref, bf16[8,256,512]{2,1,0:T(8,128)(2,1)} %collective-permute-done.6.refs_0_, ...), custom_call_target="tpu_custom_call", output_to_operand_aliasing={{}: (4, {})} | custom-call | flops 805306368 | bytes 6815744 | tf_op jit(solution)/shard_map/pallas_call | solution.py:119
  595.3 17.7 %collective-permute-done.8.refs_0_ = bf16[5,256,512]{2,1,0:T(8,128)(2,1)} collective-permute-done((bf16[5,256,512]{2,1,0:T(8,128)(2,1)}, bf16[5,256,512]{2,1,0:T(8,128)(2,1)}, u32[]{:S(2)}, u32[]{:S(2)}) %collective-permute-start.8) | collective-permute-done | bytes 1310752 | tf_op jit(solution)/shard_map/ppermute | solution.py:250
  623.2 5.5 shard_map.95.refs_1_
  630.9 12.4 %collective-permute-done.10.refs_0_ = bf16[4,256,512]{2,1,0:T(8,128)(2,1)} collective-permute-done((bf16[4,256,512]{2,1,0:T(8,128)(2,1)}, bf16[4,256,512]{2,1,0:T(8,128)(2,1)}, u32[]{:S(2)}, u32[]{:S(2)}) %collective-permute-start.10) | collective-permute-done | bytes 1048608 | tf_op jit(solution)/shard_map/ppermute | solution.py:250
  (41 shorter events, 65.3 us)
Async XLA Ops:
  1.3 12.7 %collective-permute-start = (bf16[3,384]{1,0:T(4,128)(2,1)S(1)}, bf16[3,384]{1,0:T(4,128)(2,1)S(1)}, u32[]{:S(2)}, u32[]{:S(2)}) collective-permute-start(bf16[3,384]{1,0:T(4,128)(2,1)S(1)} %slice_bitcast_fusion), channel_id=1, source_target_pairs={{0,1},{1,2},{2,3},{3,4},{4,5},{5,6},{6,7},{7,8},{8,9},{9,10},{10,1... | collective-permute-start | bytes 6920 | tf_op jit(solution)/shard_map/ppermute | solution.py:18
  3.7 10.3 %copy-start = (f32[4,384]{1,0:T(4,128)S(1)}, f32[4,384]{1,0:T(4,128)}, u32[]{:S(2)}) copy-start(f32[4,384]{1,0:T(4,128)} %refs_3_.1) | copy-start | bytes 18436
  14.0 147.3 %all-to-all-start = ((bf16[16,16,32,384]{3,2,1,0:T(8,128)(2,1)}), bf16[16,16,32,384]{3,2,1,0:T(8,128)(2,1)}, u32[]{:S(2)}, u32[]{:S(2)}) async-start(bf16[16,16,32,384]{3,2,1,0:T(8,128)(2,1)} %shard_map.76), calls=%async_computation | async-start | bytes 12582912 | tf_op jit(solution)/shard_map/all_to_all | solution.py:253
  161.3 120.2 %all-to-all-start.1 = ((bf16[16,16,32,384]{3,2,1,0:T(8,128)(2,1)}), bf16[16,16,32,384]{3,2,1,0:T(8,128)(2,1)}, u32[]{:S(2)}, u32[]{:S(2)}) async-start(bf16[16,16,32,384]{3,2,1,0:T(8,128)(2,1)} %shard_map.77), calls=%async_computation.1 | async-start | bytes 12582912 | tf_op jit(solution)/shard_map/all_to_all | solution.py:253
  186.5 93.1 %collective-permute-start.1 = (bf16[32,128,512]{2,1,0:T(8,128)(2,1)}, bf16[32,128,512]{2,1,0:T(8,128)(2,1)}, u32[]{:S(2)}, u32[]{:S(2)}) collective-permute-start(bf16[32,128,512]{2,1,0:T(8,128)(2,1)} %shard_map.78), channel_id=1, source_target_pairs={{0,16},{16,0},{1,17},{17,1},{2,18},{18,2},{3,19},{19,3},{4,20},{20... | collective-permute-start | bytes 12582920 | tf_op jit(solution)/shard_map/ppermute | solution.py:250
  281.6 140.3 %all-to-all-start.2 = ((bf16[16,13,32,384]{3,2,1,0:T(8,128)(2,1)}), bf16[16,13,32,384]{3,2,1,0:T(8,128)(2,1)}, u32[]{:S(2)}, u32[]{:S(2)}) async-start(bf16[16,13,32,384]{3,2,1,0:T(8,128)(2,1)} %slice.60), calls=%async_computation.2 | async-start | bytes 10223616 | tf_op jit(solution)/shard_map/all_to_all | solution.py:253
  328.7 93.2 %collective-permute-start.3 = (bf16[32,128,512]{2,1,0:T(8,128)(2,1)}, bf16[32,128,512]{2,1,0:T(8,128)(2,1)}, u32[]{:S(2)}, u32[]{:S(2)}) collective-permute-start(bf16[32,128,512]{2,1,0:T(8,128)(2,1)} %shard_map.79), channel_id=1, source_target_pairs={{0,16},{16,0},{1,17},{17,1},{2,18},{18,2},{3,19},{19,3},{4,20},{20... | collective-permute-start | bytes 12582920 | tf_op jit(solution)/shard_map/ppermute | solution.py:250
  358.7 13.3 %collective-permute-start.2 = (bf16[3,384]{1,0:T(4,128)(2,1)S(1)}, bf16[3,384]{1,0:T(4,128)(2,1)S(1)}, u32[]{:S(2)}, u32[]{:S(2)}) collective-permute-start(bf16[3,384]{1,0:T(4,128)(2,1)S(1)} %slice.64), channel_id=1, source_target_pairs={{1,0},{2,1},{3,2},{4,3},{5,4},{6,5},{7,6},{8,7},{9,8},{10,9},{11,1... | collective-permute-start | bytes 6920 | tf_op jit(solution)/shard_map/ppermute | solution.py:18
  421.8 83.0 %all-to-all-start.3 = ((bf16[16,9,32,384]{3,2,1,0:T(8,128)(2,1)}), bf16[16,9,32,384]{3,2,1,0:T(8,128)(2,1)}, u32[]{:S(2)}, u32[]{:S(2)}) async-start(bf16[16,9,32,384]{3,2,1,0:T(8,128)(2,1)} %slice.61), calls=%async_computation.3 | async-start | bytes 7077888 | tf_op jit(solution)/shard_map/all_to_all | solution.py:253
  434.2 70.7 %collective-permute-start.4 = (bf16[12,256,512]{2,1,0:T(8,128)(2,1)}, bf16[12,256,512]{2,1,0:T(8,128)(2,1)}, u32[]{:S(2)}, u32[]{:S(2)}) collective-permute-start(bf16[12,256,512]{2,1,0:T(8,128)(2,1)} %shard_map.82), channel_id=1, source_target_pairs={{0,16},{16,0},{1,17},{17,1},{2,18},{18,2},{3,19},{19,3},{4,20},{20... | collective-permute-start | bytes 9437192 | tf_op jit(solution)/shard_map/ppermute | solution.py:250
  504.9 62.9 %all-to-all-start.4 = ((bf16[16,6,32,384]{3,2,1,0:T(8,128)(2,1)}), bf16[16,6,32,384]{3,2,1,0:T(8,128)(2,1)}, u32[]{:S(2)}, u32[]{:S(2)}) async-start(bf16[16,6,32,384]{3,2,1,0:T(8,128)(2,1)} %slice.62), calls=%async_computation.4 | async-start | bytes 4718592 | tf_op jit(solution)/shard_map/all_to_all | solution.py:253
  511.0 8.9 %collective-permute-start.5 = (bf16[1,256,512]{2,1,0:T(8,128)(2,1)}, bf16[1,256,512]{2,1,0:T(8,128)(2,1)}, u32[]{:S(2)}, u32[]{:S(2)}) collective-permute-start(bf16[1,256,512]{2,1,0:T(8,128)(2,1)} %shard_map.83), channel_id=1, source_target_pairs={{0,16},{16,0},{1,17},{17,1},{2,18},{18,2},{3,19},{19,3},{4,20},{20... | collective-permute-start | bytes 786440 | tf_op jit(solution)/shard_map/ppermute | solution.py:250
  519.9 47.9 %collective-permute-start.6 = (bf16[8,256,512]{2,1,0:T(8,128)(2,1)}, bf16[8,256,512]{2,1,0:T(8,128)(2,1)}, u32[]{:S(2)}, u32[]{:S(2)}) collective-permute-start(bf16[8,256,512]{2,1,0:T(8,128)(2,1)} %shard_map.86), channel_id=1, source_target_pairs={{0,16},{16,0},{1,17},{17,1},{2,18},{18,2},{3,19},{19,3},{4,20},{20... | collective-permute-start | bytes 6291464 | tf_op jit(solution)/shard_map/ppermute | solution.py:250
  567.8 45.3 %all-to-all-start.5 = ((bf16[16,4,32,384]{3,2,1,0:T(8,128)(2,1)}), bf16[16,4,32,384]{3,2,1,0:T(8,128)(2,1)}, u32[]{:S(2)}, u32[]{:S(2)}) async-start(bf16[16,4,32,384]{3,2,1,0:T(8,128)(2,1)} %slice.63), calls=%async_computation.5 | async-start | bytes 3145728 | tf_op jit(solution)/shard_map/all_to_all | solution.py:253
  573.6 8.9 %collective-permute-start.7 = (bf16[1,256,512]{2,1,0:T(8,128)(2,1)}, bf16[1,256,512]{2,1,0:T(8,128)(2,1)}, u32[]{:S(2)}, u32[]{:S(2)}) collective-permute-start(bf16[1,256,512]{2,1,0:T(8,128)(2,1)} %shard_map.87), channel_id=1, source_target_pairs={{0,16},{16,0},{1,17},{17,1},{2,18},{18,2},{3,19},{19,3},{4,20},{20... | collective-permute-start | bytes 786440 | tf_op jit(solution)/shard_map/ppermute | solution.py:250
  582.5 30.5 %collective-permute-start.8 = (bf16[5,256,512]{2,1,0:T(8,128)(2,1)}, bf16[5,256,512]{2,1,0:T(8,128)(2,1)}, u32[]{:S(2)}, u32[]{:S(2)}) collective-permute-start(bf16[5,256,512]{2,1,0:T(8,128)(2,1)} %shard_map.89), channel_id=1, source_target_pairs={{0,16},{16,0},{1,17},{17,1},{2,18},{18,2},{3,19},{19,3},{4,20},{20... | collective-permute-start | bytes 3932168 | tf_op jit(solution)/shard_map/ppermute | solution.py:250
  613.1 7.2 %collective-permute-start.9 = (bf16[1,256,512]{2,1,0:T(8,128)(2,1)}, bf16[1,256,512]{2,1,0:T(8,128)(2,1)}, u32[]{:S(2)}, u32[]{:S(2)}) collective-permute-start(bf16[1,256,512]{2,1,0:T(8,128)(2,1)} %shard_map.90), channel_id=1, source_target_pairs={{0,16},{16,0},{1,17},{17,1},{2,18},{18,2},{3,19},{19,3},{4,20},{20... | collective-permute-start | bytes 786440 | tf_op jit(solution)/shard_map/ppermute | solution.py:250
  620.2 23.1 %collective-permute-start.10 = (bf16[4,256,512]{2,1,0:T(8,128)(2,1)}, bf16[4,256,512]{2,1,0:T(8,128)(2,1)}, u32[]{:S(2)}, u32[]{:S(2)}) collective-permute-start(bf16[4,256,512]{2,1,0:T(8,128)(2,1)} %shard_map.93), channel_id=1, source_target_pairs={{0,16},{16,0},{1,17},{17,1},{2,18},{18,2},{3,19},{19,3},{4,20},{20... | collective-permute-start | bytes 3145736 | tf_op jit(solution)/shard_map/ppermute | solution.py:250
